TPU v7x, 32 devices: a whole 2x2x4 slice. The times are simulated.
32 devices in a mesh: grp: 4 (over z), tile: 8 (over y, x, core).
Axes of the slice: x: 2, y: 2, z: 4, core: 2. Of those that a mesh axis runs over, the one named last changes fastest.
Arguments:
- speed: float32 [32, 2, 32, 128], P('tile'), may hold values from 0.15 to 0.4
- density: float32 [32, 2, 32, 128], P('tile'), may hold values from 1 to 3
- fwd_state: bfloat16 [32, 4, 8, 32, 128], P(('grp', 'tile')), may hold values from -6 to 6
- adj_state: bfloat16 [32, 4, 8, 32, 128], P(('grp', 'tile')), may hold values from -6 to 6
- aperture: int32 [32, 4], P(('grp', 'tile')), may hold values from 0 to 31, as said below
- src_pos: int32 [32, 3], P(('grp', 'tile')), may hold values from 0 to 127, as said below
- wavelet: float32 [32, 4], P(('grp', 'tile')), may hold values from -15 to 15
- rec_pos: int32 [32, 8, 2], P(('grp', 'tile')), may hold values from 0 to 127, as said below
- residual: float32 [32, 4, 8], P(('grp', 'tile')), may hold values from -6 to 6
Outputs:
- grad_speed: float32 [32, 2, 32, 128], P('tile')
- grad_density: float32 [32, 2, 32, 128], P('tile')
Inputs may be any that keep to these rules, and one draw needn't show every extreme that they name: `aperture`: row s is (c + j) * 4 + e for j = 0 .. 3, with one c in 0 .. 4 and one e in 0 .. 3 for each shot, so a shot takes exactly one tile from each of 4 owners. `src_pos`: columns are x in 0 .. 7, y in 0 .. 31, z in 0 .. 127. `rec_pos`: columns are y in 0 .. 31 and z in 0 .. 127.
All inputs are finite; a program needn't handle non-finite values.
Results may differ from a plain program's by a relative error of at most 0.0003.
Values sent between devices are 32-bit elements; how exact they have to be, the bound alone decides.
No kernel may reach another device: no remote copies, remote signals or barrier semaphores. Data moves between devices by JAX's collectives and lax.ppermute only.
A program may use at most 64 MiB of HBM per device.

v0:
```python
import math

import jax
import jax.numpy as jnp
from jax import lax
from jax.sharding import PartitionSpec as P

COEF = (1225.0 / 1024.0, -245.0 / 3072.0, 49.0 / 5120.0, -5.0 / 7168.0)


def padded_along(values, which_dim):
    widths = [(0, 0), (0, 0), (0, 0)]
    widths[which_dim] = (4, 4)
    return jnp.pad(values, widths)


def forward_diff(values, which_dim):
    length = values.shape[which_dim]
    padded = padded_along(values, which_dim)
    total = jnp.zeros_like(values)
    for order in range(1, 5):
        upper = lax.slice_in_dim(padded, 4 + order, 4 + order + length, axis=which_dim)
        lower = lax.slice_in_dim(padded, 5 - order, 5 - order + length, axis=which_dim)
        total = total + COEF[order - 1] * (upper - lower)
    return total


def backward_diff(values, which_dim):
    length = values.shape[which_dim]
    padded = padded_along(values, which_dim)
    total = jnp.zeros_like(values)
    for order in range(1, 5):
        upper = lax.slice_in_dim(padded, 3 + order, 3 + order + length, axis=which_dim)
        lower = lax.slice_in_dim(padded, 4 - order, 4 - order + length, axis=which_dim)
        total = total + COEF[order - 1] * (upper - lower)
    return total


def advance(pressure, velocity, bulk, buoyancy, source):
    moved = tuple(
        (
            velocity[which_dim] + buoyancy * forward_diff(pressure, which_dim)
            for which_dim in range(3)
        )
    )
    divergence = (
        backward_diff(moved[0], 0) + backward_diff(moved[1], 1) + backward_diff(moved[2], 2)
    )
    return (pressure + bulk * divergence + source, moved)


def evolve(speed_ap, density_ap, fwd_state, adj_state, src_pos, wavelet, rec_pos, residual):
    bulk = density_ap * speed_ap * speed_ap
    buoyancy = 1.0 / density_ap
    xs_cells = jnp.arange(speed_ap.shape[0], dtype=jnp.int32)
    ys_cells = jnp.arange(speed_ap.shape[1], dtype=jnp.int32)
    zs_cells = jnp.arange(speed_ap.shape[2], dtype=jnp.int32)
    src_mask = (
        (xs_cells == src_pos[0])[:, None, None]
        & (ys_cells == src_pos[1])[None, :, None]
        & (zs_cells == src_pos[2])[None, None, :]
    ).astype(jnp.float32)
    rec_mask = (
        (ys_cells[None, :, None] == rec_pos[:, 0][:, None, None])
        & (zs_cells[None, None, :] == rec_pos[:, 1][:, None, None])
    ).astype(jnp.float32)
    state = fwd_state.astype(jnp.float32)
    pressure = state[0]
    velocity = (state[1], state[2], state[3])
    changes = []
    steps_count = wavelet.shape[0]
    for step_index in range(steps_count):
        new_pressure, new_velocity = advance(
            pressure, velocity, bulk, buoyancy, wavelet[step_index] * src_mask
        )
        changes.append(
            (new_pressure - pressure, tuple((new_velocity[d] - velocity[d] for d in range(3))))
        )
        pressure, velocity = (new_pressure, new_velocity)
    adjoint = adj_state.astype(jnp.float32)
    adj_pressure = adjoint[0]
    adj_velocity = (adjoint[1], adjoint[2], adjoint[3])
    bulk_image = jnp.zeros_like(bulk)
    buoy_image = jnp.zeros_like(bulk)
    for step_index in reversed(range(steps_count)):
        adj_pressure, adj_velocity = advance(
            adj_pressure,
            adj_velocity,
            bulk,
            buoyancy,
            residual[step_index][:, None, None] * rec_mask,
        )
        bulk_image = bulk_image + changes[step_index][0] * adj_pressure
        dvel = changes[step_index][1]
        buoy_image = (
            buoy_image
            + dvel[0] * adj_velocity[0]
            + dvel[1] * adj_velocity[1]
            + dvel[2] * adj_velocity[2]
        )
    return (bulk_image, buoy_image)


def per_device(speed, density, fwd_state, adj_state, aperture, src_pos, wavelet, rec_pos, residual):
    owners = lax.axis_size("tile")
    myself = lax.axis_index("tile")
    held = speed.shape[0]
    tile_x, tile_y, depth = (speed.shape[1], speed.shape[2], speed.shape[3])
    stripes = aperture.shape[1]
    mine = aperture[0]
    lists = lax.all_gather(aperture, "tile", axis=0, tiled=True)
    owner_ids = jnp.arange(owners, dtype=jnp.int32)
    held_ids = jnp.arange(held, dtype=jnp.int32)
    matches = (lists // held == myself)[:, :, None] & (
        (lists % held)[:, :, None] == held_ids[None, None, :]
    )
    picked = jnp.sum(matches.astype(jnp.float32), axis=1)
    placed = (mine[:, None] // held == owner_ids[None, :]).astype(jnp.float32)
    highest = lax.Precision.HIGHEST
    pieces = (
        lax.all_gather(speed, "tile", axis=0, tiled=True),
        lax.all_gather(density, "tile", axis=0, tiled=True),
    )
    rows = pieces[0].shape[0]
    select = (mine[:, None] == jnp.arange(rows, dtype=jnp.int32)[None, :]).astype(jnp.float32)
    ap_speed = jnp.einsum("jt,txyz->jxyz", select, pieces[0], precision=highest)
    ap_density = jnp.einsum("jt,txyz->jxyz", select, pieces[1], precision=highest)
    speed_ap = ap_speed.reshape(stripes * tile_x, tile_y, depth)
    density_ap = ap_density.reshape(stripes * tile_x, tile_y, depth)
    bulk_image, buoy_image = evolve(
        speed_ap,
        density_ap,
        fwd_state[0],
        adj_state[0],
        src_pos[0],
        wavelet[0],
        rec_pos[0],
        residual[0],
    )
    bulk_parts = bulk_image.reshape(stripes, tile_x, tile_y, depth)
    buoy_parts = buoy_image.reshape(stripes, tile_x, tile_y, depth)
    back_bulk = jnp.einsum("jo,jxyz->oxyz", placed, bulk_parts, precision=highest)
    back_buoy = jnp.einsum("jo,jxyz->oxyz", placed, buoy_parts, precision=highest)
    came_bulk, came_buoy = (
        lax.all_to_all(back_bulk, "tile", split_axis=0, concat_axis=0, tiled=True),
        lax.all_to_all(back_buoy, "tile", split_axis=0, concat_axis=0, tiled=True),
    )
    own_bulk = jnp.einsum("rt,rxyz->txyz", picked, came_bulk, precision=highest)
    own_buoy = jnp.einsum("rt,rxyz->txyz", picked, came_buoy, precision=highest)
    bulk_sum, buoy_sum = lax.psum((own_bulk, own_buoy), "grp")
    scale = 1.0 / math.sqrt(lax.axis_size("grp") * owners)
    grad_speed = scale * (bulk_sum * (2.0 * density * speed))
    grad_density = scale * (bulk_sum * (speed * speed) - buoy_sum / (density * density))
    return (grad_speed, grad_density)


def solution(mesh):
    return jax.shard_map(
        per_device,
        mesh=mesh,
        in_specs=(
            P("tile", None, None, None),
            P("tile", None, None, None),
            P(("grp", "tile"), None, None, None, None),
            P(("grp", "tile"), None, None, None, None),
            P(("grp", "tile"), None),
            P(("grp", "tile"), None),
            P(("grp", "tile"), None),
            P(("grp", "tile"), None, None),
            P(("grp", "tile"), None, None),
        ),
        out_specs=(P("tile", None, None, None), P("tile", None, None, None)),
        check_vma=False,
    )
```

profile of v0, /device:TPU:0, one launch (start us, length us, event | category | flops | bytes accessed | tf_op | source)
XLA Modules:
  0.0 138.3 jit_solution(10093174043204132675)
XLA Ops:
  7.2 0.0 copy-start.2
  7.2 0.0 all-gather.4.cloned.1.call-start
  7.2 0.7 all-gather.4.cloned.1.call-update
  7.9 0.0 all-gather.6.cloned.1.call-start
  8.0 0.7 all-gather.6.cloned.1.call-update
  8.7 0.0 copy-done.2
  8.7 0.0 copy-start.3
  8.7 0.1 convert_element_type.67
  8.7 0.9 copy-done.3
  9.6 0.0 copy-start.6
  9.7 0.6 copy-done.6
  10.3 0.6 fusion.657
  10.9 0.6 iota_compare_fusion.6
  11.4 0.7 iota_compare_fusion.7
  12.1 0.0 copy-start.4
  12.1 0.7 iota_compare_fusion.5
  12.8 0.0 copy-done.4
  12.8 0.7 fusion.656
  13.4 0.0 copy-start.5
  13.5 0.7 copy-done.5
  14.1 10.2 %all-gather = s32[8,1,4]{2,1,0:T(1,128)S(1)} all-gather(s32[1,1,4]{2,1,0:T(1,128)S(1)} %bitcast.169), channel_id=1, replica_groups=mesh['grp'=4,'tile'=8] {'tile'}, dimensions={0}, use_global_device_ids=true | all-gather | bytes 144 | tf_op jit(solution)/shard_map/all_gather | solution.py:111
  24.3 0.1 copy.60
  24.4 0.0 copy-start.8
  24.4 0.7 copy-done.8
  25.1 0.1 iota_compare_fusion.1
  25.2 0.0 copy-start.7
  25.2 0.1 iota_compare_fusion.2
  25.3 0.1 broadcast_and_fusion
  25.3 0.5 copy-done.7
  25.9 10.2 %all-gather.4.cloned.1.call-done = f32[32,2,32,128]{3,2,1,0:T(8,128)} async-done(((f32[4,2,32,128]{3,2,1,0:T(8,128)}), f32[32,2,32,128]{3,2,1,0:T(8,128)}) %all-gather.4.cloned.1.call-update) | async-done | bytes 1048592 | tf_op jit(solution)/shard_map/all_gather | solution.py:122
  36.1 2.2 %fusion.2 = f32[4,2,32,128]{3,0,2,1:T(4,128)S(1)} fusion(f32[32,2,32,128]{3,2,1,0:T(8,128)} %all-gather.4.cloned.1.call-done, s32[4]{0:T(128)S(1)} %bitcast.170), kind=kOutput, calls=%fused_computation.2 | convolution fusion | flops 12583040 | bytes 1179664 | tf_op jit(solution)/shard_map/jt,txyz->jxyz/dot_general | solution.py:127
  38.4 23.2 %all-gather.6.cloned.1.call-done = f32[32,2,32,128]{3,2,1,0:T(8,128)} async-done(((f32[4,2,32,128]{3,2,1,0:T(8,128)}), f32[32,2,32,128]{3,2,1,0:T(8,128)}) %all-gather.6.cloned.1.call-update) | async-done | bytes 1048592 | tf_op jit(solution)/shard_map/all_gather | solution.py:121
  61.5 2.2 %fusion = f32[4,2,32,128]{3,0,2,1:T(4,128)S(1)} fusion(f32[32,2,32,128]{3,2,1,0:T(8,128)} %all-gather.6.cloned.1.call-done, s32[4]{0:T(128)S(1)} %bitcast.171), kind=kOutput, calls=%fused_computation | convolution fusion | flops 12583040 | bytes 1179664 | tf_op jit(solution)/shard_map/jt,txyz->jxyz/dot_general | solution.py:126
  63.8 0.6 fusion.468
  64.3 0.9 fusion.30
  65.2 0.4 fusion.151
  65.6 0.6 fusion.492
  66.2 0.4 fusion.180
  66.5 1.0 fusion.59
  67.5 0.6 fusion.540
  68.1 0.4 fusion.209
  68.5 1.0 fusion.88
  69.5 0.8 multiply_add_fusion
  70.3 1.3 fusion.122
  71.6 0.4 fusion.632
  72.0 0.8 copy.66
  72.8 3.4 %all-to-all-start = ((f32[8,2,32,128]{3,2,1,0:T(8,128)}), f32[8,2,32,128]{3,2,1,0:T(8,128)S(1)}, u32[]{:S(2)}, u32[]{:S(2)}) async-start(f32[8,2,32,128]{3,2,1,0:T(8,128)} %copy.66), calls=%async_computation | async-start | bytes 524288 | tf_op jit(solution)/shard_map/all_to_all | solution.py:145
  76.2 0.4 fusion.630
  76.6 0.8 copy.73
  77.4 5.7 %all-to-all-done = f32[8,2,32,128]{3,2,1,0:T(8,128)S(1)} async-done(((f32[8,2,32,128]{3,2,1,0:T(8,128)}), f32[8,2,32,128]{3,2,1,0:T(8,128)S(1)}, u32[]{:S(2)}, u32[]{:S(2)}) %all-to-all-start) | async-done | bytes 262176 | tf_op jit(solution)/shard_map/all_to_all | solution.py:145
  83.1 3.4 %all-to-all-start.1 = ((f32[8,2,32,128]{3,2,1,0:T(8,128)}), f32[8,2,32,128]{3,2,1,0:T(8,128)S(1)}, u32[]{:S(2)}, u32[]{:S(2)}) async-start(f32[8,2,32,128]{3,2,1,0:T(8,128)} %copy.73), calls=%async_computation.1 | async-start | bytes 524288 | tf_op jit(solution)/shard_map/all_to_all | solution.py:146
  86.5 0.0 all-reduce.51.cloned.1.call-start
  86.5 1.1 fusion.6
  87.7 5.7 %all-to-all-done.1 = f32[8,2,32,128]{3,2,1,0:T(8,128)S(1)} async-done(((f32[8,2,32,128]{3,2,1,0:T(8,128)}), f32[8,2,32,128]{3,2,1,0:T(8,128)S(1)}, u32[]{:S(2)}, u32[]{:S(2)}) %all-to-all-start.1) | async-done | bytes 262176 | tf_op jit(solution)/shard_map/all_to_all | solution.py:146
  93.3 1.1 fusion.4
  94.5 0.0 copy-start
  94.5 0.0 copy-start.1
  94.5 0.0 all-reduce.51.cloned.1.call-update
  94.5 34.8 %all-reduce.51.cloned.1.call-done = (f32[4,2,32,128]{3,0,2,1:T(4,128)}, f32[4,2,32,128]{3,0,2,1:T(4,128)}) async-done(((f32[4,2,32,128]{3,0,2,1:T(4,128)}, f32[4,2,32,128]{3,0,2,1:T(4,128)}), (f32[4,2,32,128]{3,0,2,1:T(4,128)}, f32[4,2,32,128]{3,0,2,1:T(4,128)})) %all-reduce.51.cloned.1.call-update) | async-done | bytes 262160 | tf_op jit(solution)/shard_map/psum | solution.py:150
  129.3 0.0 copy-done
  129.3 0.0 copy-done.1
  129.3 1.2 subtract_multiply_fusion
  130.5 0.7 copy.77
  131.2 0.7 copy.78
  (10 shorter events, 0.1 us)
Async XLA Ops:
  7.2 1.5 %copy-start.2 = (bf16[1,4,8,32,128]{4,3,2,1,0:T(8,128)(2,1)S(1)}, bf16[1,4,8,32,128]{4,3,2,1,0:T(8,128)(2,1)}, u32[]{:S(2)}) copy-start(bf16[1,4,8,32,128]{4,3,2,1,0:T(8,128)(2,1)} %param.11) | copy-start | bytes 786436
  7.2 29.0 %all-gather.4.cloned.1.call-start = ((), (), s32[]{:S(2)}) async-start(), calls=%async_computation.2 | async-start | bytes 1179648 | tf_op jit(solution)/shard_map/all_gather | solution.py:122
  7.9 53.6 %all-gather.6.cloned.1.call-start = ((), (), s32[]{:S(2)}) async-start(), calls=%async_computation.3 | async-start | bytes 1179648 | tf_op jit(solution)/shard_map/all_gather | solution.py:121
  8.7 1.0 copy-start.3
  9.6 0.7 copy-start.6
  12.1 0.7 copy-start.4
  13.4 0.7 copy-start.5
  24.4 0.7 copy-start.8
  25.2 0.7 copy-start.7
  72.8 10.3 %all-to-all-start = ((f32[8,2,32,128]{3,2,1,0:T(8,128)}), f32[8,2,32,128]{3,2,1,0:T(8,128)S(1)}, u32[]{:S(2)}, u32[]{:S(2)}) async-start(f32[8,2,32,128]{3,2,1,0:T(8,128)} %copy.66), calls=%async_computation | async-start | bytes 524288 | tf_op jit(solution)/shard_map/all_to_all | solution.py:145
  83.1 10.3 %all-to-all-start.1 = ((f32[8,2,32,128]{3,2,1,0:T(8,128)}), f32[8,2,32,128]{3,2,1,0:T(8,128)S(1)}, u32[]{:S(2)}, u32[]{:S(2)}) async-start(f32[8,2,32,128]{3,2,1,0:T(8,128)} %copy.73), calls=%async_computation.1 | async-start | bytes 524288 | tf_op jit(solution)/shard_map/all_to_all | solution.py:146
  86.5 42.8 %all-reduce.51.cloned.1.call-start = ((), (), s32[]{:S(2)}) async-start(), calls=%async_computation.4 | async-start | bytes 524288 | tf_op jit(solution)/shard_map/psum | solution.py:150
  94.5 34.8 %copy-start = (f32[4,2,32,128]{3,2,1,0:T(8,128)S(1)}, f32[4,2,32,128]{3,2,1,0:T(8,128)}, u32[]{:S(2)}) copy-start(f32[4,2,32,128]{3,2,1,0:T(8,128)} %param.10) | copy-start | bytes 393220
  94.5 34.8 %copy-start.1 = (f32[4,2,32,128]{3,2,1,0:T(8,128)S(1)}, f32[4,2,32,128]{3,2,1,0:T(8,128)}, u32[]{:S(2)}) copy-start(f32[4,2,32,128]{3,2,1,0:T(8,128)} %param.9) | copy-start | bytes 393220
Sparse Core Ops, SparseCore 0:
  9.9 26.1 all-gather.3
  38.0 23.4 all-gather.5
  94.6 34.6 all-reduce.50
where the time goes:
time: 139 us; the launch traced here: 138 us
  waiting for transfers between devices  81 us (58%)
  between operations  14 us (10%)
  other arithmetic  11.3 us (8%)
  blocking collectives  10.2 us (7%)
  local copies, waits for them, and re-layouts  7.57 us (5%)
  matrix products  7.49 us (5%)
  starting transfers between devices  6.94 us (5%)
    psum x1, waiting for transfers between devices, per_device(): bulk_sum, buoy_sum = lax.psum((own_bulk, own_buoy), 'grp')  34.8 us
    all_gather x1, waiting for transfers between devices, per_device(): lax.all_gather(speed, 'tile', axis=0, tiled=True)  23.2 us
    all_gather x1, waiting for transfers between devices, per_device(): lax.all_gather(density, 'tile', axis=0, tiled=True)  10.2 us
    all_gather x1, blocking collectives, per_device(): lists = lax.all_gather(aperture, 'tile', axis=0, tiled=True)  10.2 us
    all_to_all x1, waiting for transfers between devices, per_device(): lax.all_to_all(back_bulk, 'tile', split_axis=0, concat_axis=0, tiled=True)  5.7 us
    all_to_all x1, waiting for transfers between devices, per_device(): lax.all_to_all(back_buoy, 'tile', split_axis=0, concat_axis=0, tiled=True)  5.69 us
    unnamed x20, local copies, waits for them, and re-layouts  4.69 us
    add x6, other arithmetic, advance(): return (pressure + bulk * divergence + source, moved)  3.99 us
  transfers between devices with their start and end apart: 5, of which 5 were waited for; matrix products, arithmetic and copies ran while one was open for 6% of the time, Pallas kernels for 0%

commit v1 on v0

v1 whole, which is shorter than its diff:
```python
import functools
import math

import jax
import jax.numpy as jnp
from jax import lax
from jax.experimental import pallas as pl
from jax.experimental.pallas import tpu as pltpu
from jax.sharding import PartitionSpec as P

COEF = (1225.0 / 1024.0, -245.0 / 3072.0, 49.0 / 5120.0, -5.0 / 7168.0)
REACH = 4
EDGE = 8

VMEM = pl.BlockSpec(memory_space=pltpu.VMEM)
SMEM = pl.BlockSpec(memory_space=pltpu.SMEM)
PARAMS = pltpu.CompilerParams(vmem_limit_bytes=40 * 1024 * 1024)


def corner_and_column(list_ref, held):
    entry = list_ref[0, 0]
    return lax.div(entry, held), lax.rem(entry, held)


def pick_kernel(stripes, speed_ref, density_ref, far_speed_ref, far_density_ref, *refs):
    lists, pieces, rows = refs[:stripes], refs[stripes : 2 * stripes], refs[2 * stripes]
    held = speed_ref.shape[0]
    me = lax.axis_index("tile")
    residue, half = lax.rem(me, stripes), lax.div(me, stripes)
    for hop in range(stripes):
        corner, column = corner_and_column(lists[hop], held)
        here = (residue >= corner) == (half == 0)
        piece = pieces[hop]
        rows[hop, 0] = corner
        rows[hop, 1] = column

        @pl.when(here)
        def _():
            piece[0] = speed_ref[column]
            piece[1] = density_ref[column]

        @pl.when(jnp.logical_not(here))
        def _():
            piece[0] = far_speed_ref[column]
            piece[1] = far_density_ref[column]


def combine(ahead, behind):
    total = None
    for order in range(1, 5):
        term = COEF[order - 1] * (ahead(order) - behind(order))
        total = term if total is None else total + term
    return total


def shifted_z(values, lane, by):
    if by == 0:
        return values
    depth = values.shape[-1]
    rolled = pltpu.roll(values, (-by) % depth, axis=values.ndim - 1)
    inside = lane < depth - by if by > 0 else lane >= -by
    return jnp.where(inside, rolled, 0.0)


def wave_kernel(stripes, steps, held, *refs):
    pieces = refs[:stripes]
    (fwd_ref, adj_ref, list_ref, src_ref, wave_ref, rec_ref, res_ref) = refs[stripes : stripes + 7]
    owners = 2 * stripes
    outs = refs[stripes + 7 : stripes + 7 + owners]
    (bulk, buoy, p, v0, v1, v2, dp, dv, marks, bulk_img, buoy_img) = refs[stripes + 7 + owners :]
    tile_x = pieces[0].shape[1]
    xs, ys, zs = bulk.shape
    me = lax.axis_index("tile")
    residue = lax.rem(me, stripes)
    corner, _ = corner_and_column(list_ref, held)
    for hop in range(stripes):
        place = lax.rem((residue ^ hop) - corner + stripes, stripes)
        cells = pl.ds(place * tile_x, tile_x)
        speed, density = pieces[hop][0], pieces[hop][1]
        bulk[cells] = density * speed * speed
        buoy[cells] = 1.0 / density

    row = lax.broadcasted_iota(jnp.int32, (ys, zs), 0)
    lane = lax.broadcasted_iota(jnp.int32, (ys, zs), 1)
    src_mark = ((row == src_ref[0, 1]) & (lane == src_ref[0, 2])).astype(jnp.float32)
    for x in range(xs):
        marks[x] = ((row == rec_ref[0, x, 0]) & (lane == rec_ref[0, x, 1])).astype(jnp.float32)

    edge = jnp.zeros((REACH, ys + 2 * EDGE, zs), jnp.float32)
    p[:REACH] = edge
    p[REACH + xs :] = edge
    side = jnp.zeros((xs, EDGE, zs), jnp.float32)
    p[REACH : REACH + xs, :EDGE] = side
    p[REACH : REACH + xs, EDGE + ys :] = side
    v1[:, :EDGE] = side
    v1[:, EDGE + ys :] = side
    v0[:REACH] = edge[:, :ys]
    v0[REACH + xs :] = edge[:, :ys]
    middle = pl.ds(EDGE, ys)

    def load(state):
        for x in range(xs):
            p[REACH + x, EDGE : EDGE + ys] = state[0, 0, x].astype(jnp.float32)
            v0[REACH + x] = state[0, 1, x].astype(jnp.float32)
            v1[x, EDGE : EDGE + ys] = state[0, 2, x].astype(jnp.float32)
            v2[x] = state[0, 3, x].astype(jnp.float32)

    def slopes(x):
        centre = p[REACH + x, middle]
        along_x = combine(
            lambda k: p[REACH + x + k, middle], lambda k: p[REACH + x + 1 - k, middle]
        )
        along_y = combine(
            lambda k: p[REACH + x, pl.ds(EDGE + k, ys)],
            lambda k: p[REACH + x, pl.ds(EDGE + 1 - k, ys)],
        )
        along_z = combine(
            lambda k: shifted_z(centre, lane, k), lambda k: shifted_z(centre, lane, 1 - k)
        )
        light = buoy[x]
        return light * along_x, light * along_y, light * along_z

    def push(x):
        change = slopes(x)
        moved = (
            v0[REACH + x] + change[0],
            v1[x, middle] + change[1],
            v2[x] + change[2],
        )
        v0[REACH + x] = moved[0]
        v1[x, middle] = moved[1]
        v2[x] = moved[2]
        return change, moved

    def spread(x):
        along_x = combine(lambda k: v0[REACH + x + k - 1], lambda k: v0[REACH + x - k])
        along_y = combine(
            lambda k: v1[x, pl.ds(EDGE + k - 1, ys)], lambda k: v1[x, pl.ds(EDGE - k, ys)]
        )
        centre = v2[x]
        along_z = combine(
            lambda k: shifted_z(centre, lane, k - 1), lambda k: shifted_z(centre, lane, -k)
        )
        return bulk[x] * (along_x + along_y + along_z)

    def planes(body):
        lax.fori_loop(0, xs, lambda x, _: (body(x), 0)[1], 0, unroll=2)

    load(fwd_ref)
    for step in range(steps):

        def fwd_push(x, step=step):
            change, _ = push(x)
            for d in range(3):
                dv[step, d, x] = change[d]

        def fwd_spread(x, step=step):
            amplitude = jnp.where(x == src_ref[0, 0], wave_ref[0, step], 0.0)
            change = spread(x) + amplitude * src_mark
            dp[step, x] = change
            p[REACH + x, middle] = p[REACH + x, middle] + change

        planes(fwd_push)
        planes(fwd_spread)

    load(adj_ref)
    for step in reversed(range(steps)):
        last = step == steps - 1

        def adj_push(x, step=step, last=last):
            _, moved = push(x)
            image = dv[step, 0, x] * moved[0]
            image = image + dv[step, 1, x] * moved[1]
            image = image + dv[step, 2, x] * moved[2]
            buoy_img[x] = image if last else buoy_img[x] + image

        def adj_spread(x, step=step, last=last):
            moved = p[REACH + x, middle] + spread(x) + res_ref[0, step, x] * marks[x]
            p[REACH + x, middle] = moved
            image = dp[step, x] * moved
            bulk_img[x] = image if last else bulk_img[x] + image

        planes(adj_push)
        planes(adj_spread)

    for hop in range(owners):
        place = jnp.clip((me ^ hop) - corner, 0, stripes - 1)
        cells = pl.ds(place * tile_x, tile_x)
        outs[hop][0] = bulk_img[cells]
        outs[hop][1] = buoy_img[cells]


def gather_kernel(stripes, groups, near_ref, far_ref, *refs):
    owners = 2 * stripes
    came, parts, total = refs[:owners], refs[owners : owners + groups], refs[owners + groups]
    me, group = lax.axis_index("tile"), lax.axis_index("grp")
    tile_rows = came[0].shape[1]
    part = parts[0].shape[1]
    total[...] = jnp.zeros_like(total)
    for hop in range(owners):
        lists = near_ref if hop < stripes else far_ref
        corner, column = lists[hop % stripes, 0], lists[hop % stripes, 1]

        @pl.when((corner <= me) & (me < corner + stripes))
        def _():
            rows = pl.ds(pl.multiple_of(column * tile_rows, tile_rows), tile_rows)
            for field in range(2):
                total[field, rows] = total[field, rows] + came[hop][field]

    for hop in range(groups):
        first = pl.multiple_of(lax.rem(group + hop, groups) * part, part)
        for field in range(2):
            parts[hop][field] = total[field, pl.ds(first, part)]


def grads_kernel(scale, groups, *refs):
    parts, speed_ref, density_ref, grads = refs[:groups], *refs[groups:]
    part = parts[0].shape[1]
    rows = pl.ds(pl.multiple_of(lax.axis_index("grp") * part, part), part)
    speed, density = speed_ref[rows], density_ref[rows]
    bulk_sum, buoy_sum = parts[0][0], parts[0][1]
    for other in parts[1:]:
        bulk_sum = bulk_sum + other[0]
        buoy_sum = buoy_sum + other[1]
    grads[0] = scale * (bulk_sum * (2.0 * density * speed))
    grads[1] = scale * (bulk_sum * (speed * speed) - buoy_sum / (density * density))


def per_device(speed, density, fwd_state, adj_state, aperture, src_pos, wavelet, rec_pos, residual):
    owners = lax.axis_size("tile")
    groups = lax.axis_size("grp")
    my_group = lax.axis_index("grp")
    held, tile_x, tile_y, depth = speed.shape
    stripes = aperture.shape[1]
    steps = wavelet.shape[1]
    xs = stripes * tile_x
    f32 = jnp.float32

    def across(values, hop):
        return lax.ppermute(values, "tile", [(t, t ^ hop) for t in range(owners)])

    lists = [aperture] + [across(aperture, hop) for hop in range(1, stripes)]
    far_speed = across(speed, stripes)
    far_density = across(density, stripes)
    piece = jax.ShapeDtypeStruct((2, tile_x, tile_y, depth), f32)
    picked = pl.pallas_call(
        functools.partial(pick_kernel, stripes),
        out_shape=[piece] * stripes + [jax.ShapeDtypeStruct((stripes, 2), jnp.int32)],
        in_specs=[VMEM] * 4 + [SMEM] * stripes,
        out_specs=[VMEM] * stripes + [SMEM],
        compiler_params=PARAMS,
        name="pick_tiles",
    )(speed, density, far_speed, far_density, *lists)
    near = picked[-1]
    pieces = [picked[0]] + [across(picked[hop], hop) for hop in range(1, stripes)]
    far = across(near, stripes)

    cells = (xs, tile_y, depth)
    images = pl.pallas_call(
        functools.partial(wave_kernel, stripes, steps, held),
        out_shape=[piece] * owners,
        in_specs=[VMEM] * (stripes + 2) + [SMEM] * 5,
        out_specs=[VMEM] * owners,
        scratch_shapes=[
            pltpu.VMEM(cells, f32),
            pltpu.VMEM(cells, f32),
            pltpu.VMEM((xs + 2 * REACH, tile_y + 2 * EDGE, depth), f32),
            pltpu.VMEM((xs + 2 * REACH, tile_y, depth), f32),
            pltpu.VMEM((xs, tile_y + 2 * EDGE, depth), f32),
            pltpu.VMEM(cells, f32),
            pltpu.VMEM((steps,) + cells, f32),
            pltpu.VMEM((steps, 3) + cells, f32),
            pltpu.VMEM(cells, f32),
            pltpu.VMEM(cells, f32),
            pltpu.VMEM(cells, f32),
        ],
        compiler_params=PARAMS,
        name="replay_and_adjoint",
    )(*pieces, fwd_state, adj_state, aperture, src_pos, wavelet, rec_pos, residual)

    tile_rows = tile_x * tile_y
    rows = held * tile_rows
    part = rows // groups
    came = [images[0]] + [across(images[hop], hop) for hop in range(1, owners)]
    came = [values.reshape(2, tile_rows, depth) for values in came]
    part_shape = jax.ShapeDtypeStruct((2, part, depth), f32)
    parts = pl.pallas_call(
        functools.partial(gather_kernel, stripes, groups),
        out_shape=[part_shape] * groups,
        in_specs=[SMEM] * 2 + [VMEM] * owners,
        out_specs=[VMEM] * groups,
        scratch_shapes=[pltpu.VMEM((2, rows, depth), f32)],
        compiler_params=PARAMS,
        name="add_stripes",
    )(near, far, *came)

    def along(values, hop):
        return lax.ppermute(values, "grp", [(g, (g + hop) % groups) for g in range(groups)])

    parts = [parts[0]] + [along(parts[hop], hop) for hop in range(1, groups)]
    grads = pl.pallas_call(
        functools.partial(grads_kernel, 1.0 / math.sqrt(groups * owners), groups),
        out_shape=part_shape,
        in_specs=[VMEM] * (groups + 2),
        out_specs=VMEM,
        compiler_params=PARAMS,
        name="gradients",
    )(*parts, speed.reshape(rows, depth), density.reshape(rows, depth))

    whole = jnp.zeros((2, groups, part, depth), f32)
    for hop in range(groups):
        values = grads if hop == 0 else along(grads, hop)
        place = lax.rem(my_group - hop + groups, groups)
        whole = lax.dynamic_update_slice_in_dim(whole, values[:, None], place, axis=1)
    return (whole[0].reshape(speed.shape), whole[1].reshape(speed.shape))


def solution(mesh):
    return jax.shard_map(
        per_device,
        mesh=mesh,
        in_specs=(
            P("tile", None, None, None),
            P("tile", None, None, None),
            P(("grp", "tile"), None, None, None, None),
            P(("grp", "tile"), None, None, None, None),
            P(("grp", "tile"), None),
            P(("grp", "tile"), None),
            P(("grp", "tile"), None),
            P(("grp", "tile"), None, None),
            P(("grp", "tile"), None, None),
        ),
        out_specs=(P("tile", None, None, None), P("tile", None, None, None)),
        check_vma=False,
    )
```

time: 139 us -> 61.3 us (0.44)
  waiting for transfers between devices: 81 us -> 21.3 us
  starting transfers between devices: 6.94 us -> 24.4 us
  between operations: 14 us -> 0.77 us
  Pallas kernels: 0 us -> 11.4 us
  other arithmetic: 11.3 us -> 0 us
  blocking collectives: 10.2 us -> 0 us
  matrix products: 7.49 us -> 0 us
  local copies, waits for them, and re-layouts: 7.57 us -> 3.37 us
    psum x1 -> x0, waiting for transfers between devices: 34.8 us -> none  [per_device(): bulk_sum, buoy_sum = lax.psum((own_bulk, own_buoy), 'grp')]
    all_gather x2 -> x0, waiting for transfers between devices: 33.4 us -> none  [the longest x1 23.2 us: per_device(): lax.all_gather(speed, 'tile', axis=0, tiled=True)]
    ppermute x0 -> x22, starting transfers between devices: none -> 24.4 us  [the longest x16 14.7 us: across(): return lax.ppermute(values, 'tile', [(t, t ^ hop) for t in range(owners)])]
    ppermute x0 -> x22, waiting for transfers between devices: none -> 21.3 us  [the longest x16 13.4 us: across(): return lax.ppermute(values, 'tile', [(t, t ^ hop) for t in range(owners)])]
    all_to_all x2 -> x0, waiting for transfers between devices: 11.4 us -> none  [the longest x1 5.7 us: per_device(): lax.all_to_all(back_bulk, 'tile', split_axis=0, concat_axis=0, tiled=True)]
    pallas_call x0 -> x4, Pallas kernels: none -> 11.4 us  [the longest x1 9.38 us: per_device(): pl.pallas_call(functools.partial(wave_kernel, stripes, steps, held), out_...]
    all_gather x1 -> x0, blocking collectives: 10.2 us -> none  [per_device(): lists = lax.all_gather(aperture, 'tile', axis=0, tiled=True)]
    add x11 -> x0, other arithmetic: 7.8 us -> none  [the longest x6 3.99 us: advance(): return (pressure + bulk * divergence + source, moved)]
  transfers between devices with their start and end apart: 5 -> 22, of which waited for: 5 -> 15; matrix products, arithmetic and copies ran while one was open for 6% -> 0% of each run, Pallas kernels for 0% -> 0%
where the time goes in v1:
time: 61.3 us; the launch traced here: 61.2 us
  starting transfers between devices  24.4 us (40%)
  waiting for transfers between devices  21.3 us (35%)
  Pallas kernels  11.4 us (19%)
  local copies, waits for them, and re-layouts  3.37 us (5%)
  between operations  0.77 us (1%)
    ppermute x16, starting transfers between devices, across(): return lax.ppermute(values, 'tile', [(t, t ^ hop) for t in range(owners)])  14.7 us
    ppermute x16, waiting for transfers between devices, across(): return lax.ppermute(values, 'tile', [(t, t ^ hop) for t in range(owners)])  13.4 us
    ppermute x6, starting transfers between devices, along(): lax.ppermute(values, 'grp', [(g, (g + hop) % groups) for g in range(group...  9.71 us
    pallas_call x1, Pallas kernels, per_device(): pl.pallas_call(functools.partial(wave_kernel, stripes, steps, held), out_...  9.38 us
    ppermute x6, waiting for transfers between devices, along(): lax.ppermute(values, 'grp', [(g, (g + hop) % groups) for g in range(group...  7.88 us
    unnamed x25, local copies, waits for them, and re-layouts  2.58 us
    pallas_call x1, Pallas kernels, per_device(): pl.pallas_call(functools.partial(pick_kernel, stripes), out_shape=[piece]...  1.26 us
  transfers between devices with their start and end apart: 22, of which 15 were waited for; matrix products, arithmetic and copies ran while one was open for 0% of the time, Pallas kernels for 0%

profile of v1, /device:TPU:0, one launch (start us, length us, event | category | flops | bytes accessed | tf_op | source)
XLA Modules:
  0.0 61.2 jit_solution(14338815523855635091)
XLA Ops:
  0.6 3.0 %collective-permute-start = (f32[4,2,32,128]{3,2,1,0:T(8,128)}, f32[4,2,32,128]{3,2,1,0:T(8,128)S(1)}, u32[]{:S(2)}, u32[]{:S(2)}) collective-permute-start(f32[4,2,32,128]{3,2,1,0:T(8,128)} %speed_ref.1), channel_id=1, source_target_pairs={{0,4},{1,5},{2,6},{3,7},{4,0},{5,1},{6,2},{7,3},{8,12},{9,13},{10,... | collective-permute-start | bytes 393224 | tf_op jit(solution)/shard_map/ppermute | solution.py:240
  3.7 0.1 collective-permute-start.1
  3.7 0.0 collective-permute-start.2
  3.7 1.9 %collective-permute-start.3 = (s32[1,4]{1,0:T(1,128)}, s32[1,4]{1,0:T(1,128)S(1)}, u32[]{:S(2)}, u32[]{:S(2)}) collective-permute-start(s32[1,4]{1,0:T(1,128)} %refs_6_.1), channel_id=1, source_target_pairs={{0,2},{1,3},{2,0},{3,1},{4,6},{5,7},{6,4},{7,5},{8,10},{9,11},{10,... | collective-permute-start | bytes 56 | tf_op jit(solution)/shard_map/ppermute | solution.py:240
  5.7 0.2 collective-permute-start.4
  5.8 0.0 collective-permute-done.2.refs_1_
  5.8 1.6 %collective-permute-done.3.refs_2_ = s32[1,4]{1,0:T(1,128)S(1)} collective-permute-done((s32[1,4]{1,0:T(1,128)}, s32[1,4]{1,0:T(1,128)S(1)}, u32[]{:S(2)}, u32[]{:S(2)}) %collective-permute-start.3) | collective-permute-done | bytes 48 | tf_op jit(solution)/shard_map/ppermute | solution.py:240
  7.4 1.3 %collective-permute-done.4.refs_3_ = s32[1,4]{1,0:T(1,128)S(1)} collective-permute-done((s32[1,4]{1,0:T(1,128)}, s32[1,4]{1,0:T(1,128)S(1)}, u32[]{:S(2)}, u32[]{:S(2)}) %collective-permute-start.4) | collective-permute-done | bytes 48 | tf_op jit(solution)/shard_map/ppermute | solution.py:240
  8.8 0.0 collective-permute-done.far_speed_ref
  8.8 1.4 %collective-permute-done.1.far_density_ref = f32[4,2,32,128]{3,2,1,0:T(8,128)S(1)} collective-permute-done((f32[4,2,32,128]{3,2,1,0:T(8,128)}, f32[4,2,32,128]{3,2,1,0:T(8,128)S(1)}, u32[]{:S(2)}, u32[]{:S(2)}) %collective-permute-start.1) | collective-permute-done | bytes 131104 | tf_op jit(solution)/shard_map/ppermute | solution.py:240
  10.2 0.0 copy-start
  10.2 0.9 %copy-done = f32[4,2,32,128]{3,2,1,0:T(8,128)S(1)} copy-done((f32[4,2,32,128]{3,2,1,0:T(8,128)S(1)}, f32[4,2,32,128]{3,2,1,0:T(8,128)}, u32[]{:S(2)}) %copy-start) | copy-done | bytes 131096
  11.1 0.9 %copy-done.2 = f32[4,2,32,128]{3,2,1,0:T(8,128)S(1)} copy-done((f32[4,2,32,128]{3,2,1,0:T(8,128)S(1)}, f32[4,2,32,128]{3,2,1,0:T(8,128)}, u32[]{:S(2)}) %copy-start.2) | copy-done | bytes 131096
  12.0 0.0 copy-start.7
  12.0 0.7 %copy-done.7 = s32[1,4]{1,0:T(1,128)S(1)} copy-done((s32[1,4]{1,0:T(1,128)S(1)}, s32[1,4]{1,0:T(1,128)}, u32[]{:S(2)}) %copy-start.7) | copy-done | bytes 40
  12.7 1.3 %pick_tiles.1 = (f32[2,2,32,128]{3,2,1,0:T(8,128)S(1)}, f32[2,2,32,128]{3,2,1,0:T(8,128)S(1)}, f32[2,2,32,128]{3,2,1,0:T(8,128)S(1)}, f32[2,2,32,128]{3,2,1,0:T(8,128)S(1)}, s32[4,2]{1,0:T(4,128)S(1)}) custom-call(f32[4,2,32,128]{3,2,1,0:T(8,128)S(1)} %copy-done, f32[4,2,32,128]{3,2,1,0:T(8,128)S(1)} %copy-done.2, ...), custom_call_target="tpu_custom_call" | custom-call | tf_op jit(solution)/shard_map/pick_tiles/pallas_call | solution.py:246
  13.9 0.1 collective-permute-start.6
  14.0 0.0 copy-start.11
  14.0 1.8 %collective-permute-start.7 = (f32[2,2,32,128]{3,2,1,0:T(8,128)S(1)}, f32[2,2,32,128]{3,2,1,0:T(8,128)S(1)}, u32[]{:S(2)}, u32[]{:S(2)}) collective-permute-start(f32[2,2,32,128]{3,2,1,0:T(8,128)S(1)} %get-tuple-element.22), channel_id=1, source_target_pairs={{0,2},{1,3},{2,0},{3,1},{4,6},{5,7},{6,4},{7,5},{8,10},{9,11},{10,... | collective-permute-start | bytes 196616 | tf_op jit(solution)/shard_map/ppermute | solution.py:240
  15.8 0.1 collective-permute-start.8
  15.9 0.0 copy-done.11
  15.9 0.1 copy.11.refs_9_
  16.0 0.0 collective-permute-done.6.refs_1_
  16.0 2.5 %collective-permute-done.7.refs_2_ = f32[2,2,32,128]{3,2,1,0:T(8,128)S(1)} collective-permute-done((f32[2,2,32,128]{3,2,1,0:T(8,128)S(1)}, f32[2,2,32,128]{3,2,1,0:T(8,128)S(1)}, u32[]{:S(2)}, u32[]{:S(2)}) %collective-permute-start.7) | collective-permute-done | bytes 65568 | tf_op jit(solution)/shard_map/ppermute | solution.py:240
  18.5 1.3 %collective-permute-done.8.refs_3_ = f32[2,2,32,128]{3,2,1,0:T(8,128)S(1)} collective-permute-done((f32[2,2,32,128]{3,2,1,0:T(8,128)S(1)}, f32[2,2,32,128]{3,2,1,0:T(8,128)S(1)}, u32[]{:S(2)}, u32[]{:S(2)}) %collective-permute-start.8) | collective-permute-done | bytes 65568 | tf_op jit(solution)/shard_map/ppermute | solution.py:240
  19.8 0.0 copy-done.4
  19.8 0.0 copy-done.5
  19.8 0.0 copy-done.6
  19.8 0.0 copy-done.8
  19.9 0.0 copy-done.9
  19.9 0.0 copy-done.10
  19.9 9.4 %replay_and_adjoint.1 = (f32[2,2,32,128]{3,2,1,0:T(8,128)S(1)}, f32[2,2,32,128]{3,2,1,0:T(8,128)S(1)}, f32[2,2,32,128]{3,2,1,0:T(8,128)S(1)}, f32[2,2,32,128]{3,...) custom-call(f32[2,2,32,128]{3,2,1,0:T(8,128)S(1)} %get-tuple-element, ...), custom_call_target="tpu_custom_call" | custom-call | tf_op jit(solution)/shard_map/replay_and_adjoint/pallas_call | solution.py:259
  29.3 0.2 collective-permute-start.9
  29.5 1.4 %collective-permute-start.10 = (f32[2,2,32,128]{3,2,1,0:T(8,128)S(1)}, f32[2,2,32,128]{3,2,1,0:T(8,128)S(1)}, u32[]{:S(2)}, u32[]{:S(2)}) collective-permute-start(f32[2,2,32,128]{3,2,1,0:T(8,128)S(1)} %get-tuple-element.26), channel_id=1, source_target_pairs={{0,2},{1,3},{2,0},{3,1},{4,6},{5,7},{6,4},{7,5},{8,10},{9,11},{10,... | collective-permute-start | bytes 196616 | tf_op jit(solution)/shard_map/ppermute | solution.py:240
  30.9 1.5 %collective-permute-start.5 = (s32[4,2]{1,0:T(4,128)S(1)}, s32[4,2]{1,0:T(4,128)S(1)}, u32[]{:S(2)}, u32[]{:S(2)}) collective-permute-start(s32[4,2]{1,0:T(4,128)S(1)} %get-tuple-element.19.near_ref), channel_id=1, source_target_pairs={{0,4},{1,5},{2,6},{3,7},{4,0},{5,1},{6,2},{7,3},{8,12},{9,13},{10,... | collective-permute-start | bytes 104 | tf_op jit(solution)/shard_map/ppermute | solution.py:240
  32.5 0.0 collective-permute-start.11
  32.5 0.5 collective-permute-start.12
  33.0 1.6 %collective-permute-done.5.far_ref = s32[4,2]{1,0:T(4,128)S(1)} collective-permute-done((s32[4,2]{1,0:T(4,128)S(1)}, s32[4,2]{1,0:T(4,128)S(1)}, u32[]{:S(2)}, u32[]{:S(2)}) %collective-permute-start.5) | collective-permute-done | bytes 64 | tf_op jit(solution)/shard_map/ppermute | solution.py:240
  34.5 0.2 collective-permute-start.13
  34.7 0.0 collective-permute-done.9
  34.7 1.3 %collective-permute-start.14 = (f32[2,2,32,128]{3,2,1,0:T(8,128)S(1)}, f32[2,2,32,128]{3,2,1,0:T(8,128)S(1)}, u32[]{:S(2)}, u32[]{:S(2)}) collective-permute-start(f32[2,2,32,128]{3,2,1,0:T(8,128)S(1)} %get-tuple-element.30), channel_id=1, source_target_pairs={{0,6},{1,7},{2,4},{3,5},{4,2},{5,3},{6,0},{7,1},{8,14},{9,15},{10,... | collective-permute-start | bytes 196616 | tf_op jit(solution)/shard_map/ppermute | solution.py:240
  36.1 0.0 collective-permute-done.10
  36.1 2.3 %collective-permute-start.15 = (f32[2,2,32,128]{3,2,1,0:T(8,128)S(1)}, f32[2,2,32,128]{3,2,1,0:T(8,128)S(1)}, u32[]{:S(2)}, u32[]{:S(2)}) collective-permute-start(f32[2,2,32,128]{3,2,1,0:T(8,128)S(1)} %get-tuple-element.31), channel_id=1, source_target_pairs={{0,7},{1,6},{2,5},{3,4},{4,3},{5,2},{6,1},{7,0},{8,15},{9,14},{10,... | collective-permute-start | bytes 196616 | tf_op jit(solution)/shard_map/ppermute | solution.py:240
  38.4 0.0 collective-permute-done.11
  38.4 0.0 collective-permute-done.12
  38.4 0.4 collective-permute-done.13
  38.8 1.4 %collective-permute-done.14 = f32[2,2,32,128]{3,2,1,0:T(8,128)S(1)} collective-permute-done((f32[2,2,32,128]{3,2,1,0:T(8,128)S(1)}, f32[2,2,32,128]{3,2,1,0:T(8,128)S(1)}, u32[]{:S(2)}, u32[]{:S(2)}) %collective-permute-start.14) | collective-permute-done | bytes 65568 | tf_op jit(solution)/shard_map/ppermute | solution.py:240
  40.2 1.8 %collective-permute-done.15 = f32[2,2,32,128]{3,2,1,0:T(8,128)S(1)} collective-permute-done((f32[2,2,32,128]{3,2,1,0:T(8,128)S(1)}, f32[2,2,32,128]{3,2,1,0:T(8,128)S(1)}, u32[]{:S(2)}, u32[]{:S(2)}) %collective-permute-start.15) | collective-permute-done | bytes 65568 | tf_op jit(solution)/shard_map/ppermute | solution.py:240
  42.0 0.7 %add_stripes.1 = (f32[2,64,128]{2,1,0:T(8,128)S(1)}, f32[2,64,128]{2,1,0:T(8,128)S(1)}, f32[2,64,128]{2,1,0:T(8,128)S(1)}, f32[2,64,128]{2,1,0:T(8,128)S(1)}) custom-call(s32[4,2]{1,0:T(4,128)S(1)} %get-tuple-element.19.near_ref, s32[4,2]{1,0:T(4,128)S(1)} %collective-permute-done.5.far_ref, f32[2,64,128]{2,1,0:T(8,128)S(1)} %bitcast.24, ...), custom_call_target="tpu_custom_call" | custom-call | tf_op jit(solution)/shard_map/add_stripes/pallas_call | solution.py:287
  42.7 1.6 %collective-permute-start.16 = (f32[2,64,128]{2,1,0:T(8,128)S(1)}, f32[2,64,128]{2,1,0:T(8,128)S(1)}, u32[]{:S(2)}, u32[]{:S(2)}) collective-permute-start(f32[2,64,128]{2,1,0:T(8,128)S(1)} %get-tuple-element.33), channel_id=1, source_target_pairs={{0,8},{8,16},{16,24},{24,0},{1,9},{9,17},{17,25},{25,1},{2,10},{10... | collective-permute-start | bytes 196616 | tf_op jit(solution)/shard_map/ppermute | solution.py:298
  44.3 2.6 %collective-permute-start.17 = (f32[2,64,128]{2,1,0:T(8,128)S(1)}, f32[2,64,128]{2,1,0:T(8,128)S(1)}, u32[]{:S(2)}, u32[]{:S(2)}) collective-permute-start(f32[2,64,128]{2,1,0:T(8,128)S(1)} %get-tuple-element.34), channel_id=1, source_target_pairs={{0,16},{8,24},{16,0},{24,8},{1,17},{9,25},{17,1},{25,9},{2,18},{10... | collective-permute-start | bytes 196616 | tf_op jit(solution)/shard_map/ppermute | solution.py:298
  46.9 1.3 %collective-permute-start.18 = (f32[2,64,128]{2,1,0:T(8,128)S(1)}, f32[2,64,128]{2,1,0:T(8,128)S(1)}, u32[]{:S(2)}, u32[]{:S(2)}) collective-permute-start(f32[2,64,128]{2,1,0:T(8,128)S(1)} %get-tuple-element.35), channel_id=1, source_target_pairs={{0,24},{8,0},{16,8},{24,16},{1,25},{9,1},{17,9},{25,17},{2,26},{10... | collective-permute-start | bytes 196616 | tf_op jit(solution)/shard_map/ppermute | solution.py:298
  48.3 0.9 %collective-permute-done.16.refs_1_ = f32[2,64,128]{2,1,0:T(8,128)S(1)} collective-permute-done((f32[2,64,128]{2,1,0:T(8,128)S(1)}, f32[2,64,128]{2,1,0:T(8,128)S(1)}, u32[]{:S(2)}, u32[]{:S(2)}) %collective-permute-start.16) | collective-permute-done | bytes 65568 | tf_op jit(solution)/shard_map/ppermute | solution.py:298
  49.2 2.4 %collective-permute-done.17.refs_2_ = f32[2,64,128]{2,1,0:T(8,128)S(1)} collective-permute-done((f32[2,64,128]{2,1,0:T(8,128)S(1)}, f32[2,64,128]{2,1,0:T(8,128)S(1)}, u32[]{:S(2)}, u32[]{:S(2)}) %collective-permute-start.17) | collective-permute-done | bytes 65568 | tf_op jit(solution)/shard_map/ppermute | solution.py:298
  51.6 0.1 collective-permute-done.18.refs_3_
  51.7 0.0 copy-done.1
  51.7 0.0 copy-done.3
  51.8 1.7 %collective-permute-start.19 = (f32[2,64,128]{2,1,0:T(8,128)S(1)}, f32[2,64,128]{2,1,0:T(8,128)S(1)}, u32[]{:S(2)}, u32[]{:S(2)}) collective-permute-start(f32[2,64,128]{2,1,0:T(8,128)S(1)} %gradients.1), channel_id=1, source_target_pairs={{0,8},{8,16},{16,24},{24,0},{1,9},{9,17},{17,25},{25,1},{2,10},{10... | collective-permute-start | bytes 196616 | tf_op jit(solution)/shard_map/ppermute | solution.py:298
  53.5 1.9 %collective-permute-start.20 = (f32[2,64,128]{2,1,0:T(8,128)S(1)}, f32[2,64,128]{2,1,0:T(8,128)S(1)}, u32[]{:S(2)}, u32[]{:S(2)}) collective-permute-start(f32[2,64,128]{2,1,0:T(8,128)S(1)} %gradients.1), channel_id=1, source_target_pairs={{0,16},{8,24},{16,0},{24,8},{1,17},{9,25},{17,1},{25,9},{2,18},{10... | collective-permute-start | bytes 196616 | tf_op jit(solution)/shard_map/ppermute | solution.py:298
  55.4 0.5 collective-permute-start.21
  56.0 2.1 %collective-permute-done.19 = f32[2,64,128]{2,1,0:T(8,128)S(1)} collective-permute-done((f32[2,64,128]{2,1,0:T(8,128)S(1)}, f32[2,64,128]{2,1,0:T(8,128)S(1)}, u32[]{:S(2)}, u32[]{:S(2)}) %collective-permute-start.19) | collective-permute-done | bytes 65568 | tf_op jit(solution)/shard_map/ppermute | solution.py:298
  58.1 2.0 %collective-permute-done.20 = f32[2,64,128]{2,1,0:T(8,128)S(1)} collective-permute-done((f32[2,64,128]{2,1,0:T(8,128)S(1)}, f32[2,64,128]{2,1,0:T(8,128)S(1)}, u32[]{:S(2)}, u32[]{:S(2)}) %collective-permute-start.20) | collective-permute-done | bytes 65568 | tf_op jit(solution)/shard_map/ppermute | solution.py:298
  60.2 0.3 collective-permute-done.21
  60.4 0.7 %fusion = (f32[1,4,64,128]{3,2,1,0:T(8,128)}, f32[1,4,64,128]{3,2,1,0:T(8,128)}) fusion(f32[2,4,64,128]{3,2,1,0:T(8,128)S(1)} %bitcast_dynamic-update-slice_fusion), kind=kLoop, calls=%fused_computation.4 | loop fusion | bytes 524288 | tf_op jit(solution)/shard_map/slice | solution.py:315
  (16 shorter events, 0.1 us)
Async XLA Ops:
  0.6 8.1 %collective-permute-start = (f32[4,2,32,128]{3,2,1,0:T(8,128)}, f32[4,2,32,128]{3,2,1,0:T(8,128)S(1)}, u32[]{:S(2)}, u32[]{:S(2)}) collective-permute-start(f32[4,2,32,128]{3,2,1,0:T(8,128)} %speed_ref.1), channel_id=1, source_target_pairs={{0,4},{1,5},{2,6},{3,7},{4,0},{5,1},{6,2},{7,3},{8,12},{9,13},{10,... | collective-permute-start | bytes 393224 | tf_op jit(solution)/shard_map/ppermute | solution.py:240
  3.7 6.5 %collective-permute-start.1 = (f32[4,2,32,128]{3,2,1,0:T(8,128)}, f32[4,2,32,128]{3,2,1,0:T(8,128)S(1)}, u32[]{:S(2)}, u32[]{:S(2)}) collective-permute-start(f32[4,2,32,128]{3,2,1,0:T(8,128)} %density_ref.1), channel_id=1, source_target_pairs={{0,4},{1,5},{2,6},{3,7},{4,0},{5,1},{6,2},{7,3},{8,12},{9,13},{10,... | collective-permute-start | bytes 393224 | tf_op jit(solution)/shard_map/ppermute | solution.py:240
  3.7 2.1 %collective-permute-start.2 = (s32[1,4]{1,0:T(1,128)}, s32[1,4]{1,0:T(1,128)S(1)}, u32[]{:S(2)}, u32[]{:S(2)}) collective-permute-start(s32[1,4]{1,0:T(1,128)} %refs_6_.1), channel_id=1, source_target_pairs={{0,1},{1,0},{2,3},{3,2},{4,5},{5,4},{6,7},{7,6},{8,9},{9,8},{10,11... | collective-permute-start | bytes 56 | tf_op jit(solution)/shard_map/ppermute | solution.py:240
  3.7 3.7 %collective-permute-start.3 = (s32[1,4]{1,0:T(1,128)}, s32[1,4]{1,0:T(1,128)S(1)}, u32[]{:S(2)}, u32[]{:S(2)}) collective-permute-start(s32[1,4]{1,0:T(1,128)} %refs_6_.1), channel_id=1, source_target_pairs={{0,2},{1,3},{2,0},{3,1},{4,6},{5,7},{6,4},{7,5},{8,10},{9,11},{10,... | collective-permute-start | bytes 56 | tf_op jit(solution)/shard_map/ppermute | solution.py:240
  5.7 3.1 %collective-permute-start.4 = (s32[1,4]{1,0:T(1,128)}, s32[1,4]{1,0:T(1,128)S(1)}, u32[]{:S(2)}, u32[]{:S(2)}) collective-permute-start(s32[1,4]{1,0:T(1,128)} %refs_6_.1), channel_id=1, source_target_pairs={{0,3},{1,2},{2,1},{3,0},{4,7},{5,6},{6,5},{7,4},{8,11},{9,10},{10,... | collective-permute-start | bytes 56 | tf_op jit(solution)/shard_map/ppermute | solution.py:240
  10.2 0.9 %copy-start = (f32[4,2,32,128]{3,2,1,0:T(8,128)S(1)}, f32[4,2,32,128]{3,2,1,0:T(8,128)}, u32[]{:S(2)}) copy-start(f32[4,2,32,128]{3,2,1,0:T(8,128)} %speed_ref.1) | copy-start | bytes 393220
  11.1 0.9 %copy-start.2 = (f32[4,2,32,128]{3,2,1,0:T(8,128)S(1)}, f32[4,2,32,128]{3,2,1,0:T(8,128)}, u32[]{:S(2)}) copy-start(f32[4,2,32,128]{3,2,1,0:T(8,128)} %density_ref.1) | copy-start | bytes 393220
  12.0 0.7 %copy-start.7 = (s32[1,4]{1,0:T(1,128)S(1)}, s32[1,4]{1,0:T(1,128)}, u32[]{:S(2)}) copy-start(s32[1,4]{1,0:T(1,128)} %refs_6_.1) | copy-start | bytes 52
  12.6 7.2 %copy-start.4 = (bf16[1,4,8,32,128]{4,3,2,1,0:T(8,128)(2,1)S(1)}, bf16[1,4,8,32,128]{4,3,2,1,0:T(8,128)(2,1)}, u32[]{:S(2)}) copy-start(bf16[1,4,8,32,128]{4,3,2,1,0:T(8,128)(2,1)} %refs_4_.1) | copy-start | bytes 786436
  12.6 7.2 %copy-start.5 = (bf16[1,4,8,32,128]{4,3,2,1,0:T(8,128)(2,1)S(1)}, bf16[1,4,8,32,128]{4,3,2,1,0:T(8,128)(2,1)}, u32[]{:S(2)}) copy-start(bf16[1,4,8,32,128]{4,3,2,1,0:T(8,128)(2,1)} %refs_5_.1) | copy-start | bytes 786436
  13.9 2.0 %collective-permute-start.6 = (f32[2,2,32,128]{3,2,1,0:T(8,128)S(1)}, f32[2,2,32,128]{3,2,1,0:T(8,128)S(1)}, u32[]{:S(2)}, u32[]{:S(2)}) collective-permute-start(f32[2,2,32,128]{3,2,1,0:T(8,128)S(1)} %get-tuple-element.21), channel_id=1, source_target_pairs={{0,1},{1,0},{2,3},{3,2},{4,5},{5,4},{6,7},{7,6},{8,9},{9,8},{10,11... | collective-permute-start | bytes 196616 | tf_op jit(solution)/shard_map/ppermute | solution.py:240
  14.0 1.9 %copy-start.11 = (s32[1,8,2]{1,2,0:T(2,128)S(1)}, s32[1,8,2]{1,2,0:T(2,128)}, u32[]{:S(2)}) copy-start(s32[1,8,2]{1,2,0:T(2,128)} %param.16) | copy-start | bytes 196
  14.0 4.5 %collective-permute-start.7 = (f32[2,2,32,128]{3,2,1,0:T(8,128)S(1)}, f32[2,2,32,128]{3,2,1,0:T(8,128)S(1)}, u32[]{:S(2)}, u32[]{:S(2)}) collective-permute-start(f32[2,2,32,128]{3,2,1,0:T(8,128)S(1)} %get-tuple-element.22), channel_id=1, source_target_pairs={{0,2},{1,3},{2,0},{3,1},{4,6},{5,7},{6,4},{7,5},{8,10},{9,11},{10,... | collective-permute-start | bytes 196616 | tf_op jit(solution)/shard_map/ppermute | solution.py:240
  15.8 4.1 %collective-permute-start.8 = (f32[2,2,32,128]{3,2,1,0:T(8,128)S(1)}, f32[2,2,32,128]{3,2,1,0:T(8,128)S(1)}, u32[]{:S(2)}, u32[]{:S(2)}) collective-permute-start(f32[2,2,32,128]{3,2,1,0:T(8,128)S(1)} %get-tuple-element.23), channel_id=1, source_target_pairs={{0,3},{1,2},{2,1},{3,0},{4,7},{5,6},{6,5},{7,4},{8,11},{9,10},{10,... | collective-permute-start | bytes 196616 | tf_op jit(solution)/shard_map/ppermute | solution.py:240
  15.9 4.0 %copy-start.6 = (f32[1,4,8]{2,1,0:T(4,128)S(1)}, f32[1,4,8]{2,1,0:T(4,128)}, u32[]{:S(2)}) copy-start(f32[1,4,8]{2,1,0:T(4,128)} %refs_10_.1) | copy-start | bytes 388
  15.9 3.9 %copy-start.8 = (s32[1,4]{1,0:T(1,128)S(1)}, s32[1,4]{1,0:T(1,128)}, u32[]{:S(2)}) copy-start(s32[1,4]{1,0:T(1,128)} %refs_6_.1) | copy-start | bytes 52
  15.9 3.9 %copy-start.9 = (s32[1,3]{1,0:T(1,128)S(1)}, s32[1,3]{1,0:T(1,128)}, u32[]{:S(2)}) copy-start(s32[1,3]{1,0:T(1,128)} %refs_7_.1) | copy-start | bytes 40
  16.0 3.9 %copy-start.10 = (f32[1,4]{1,0:T(1,128)S(1)}, f32[1,4]{1,0:T(1,128)}, u32[]{:S(2)}) copy-start(f32[1,4]{1,0:T(1,128)} %refs_8_.1) | copy-start | bytes 52
  29.3 5.5 %collective-permute-start.9 = (f32[2,2,32,128]{3,2,1,0:T(8,128)S(1)}, f32[2,2,32,128]{3,2,1,0:T(8,128)S(1)}, u32[]{:S(2)}, u32[]{:S(2)}) collective-permute-start(f32[2,2,32,128]{3,2,1,0:T(8,128)S(1)} %get-tuple-element.25), channel_id=1, source_target_pairs={{0,1},{1,0},{2,3},{3,2},{4,5},{5,4},{6,7},{7,6},{8,9},{9,8},{10,11... | collective-permute-start | bytes 196616 | tf_op jit(solution)/shard_map/ppermute | solution.py:240
  29.5 6.6 %collective-permute-start.10 = (f32[2,2,32,128]{3,2,1,0:T(8,128)S(1)}, f32[2,2,32,128]{3,2,1,0:T(8,128)S(1)}, u32[]{:S(2)}, u32[]{:S(2)}) collective-permute-start(f32[2,2,32,128]{3,2,1,0:T(8,128)S(1)} %get-tuple-element.26), channel_id=1, source_target_pairs={{0,2},{1,3},{2,0},{3,1},{4,6},{5,7},{6,4},{7,5},{8,10},{9,11},{10,... | collective-permute-start | bytes 196616 | tf_op jit(solution)/shard_map/ppermute | solution.py:240
  30.9 3.6 %collective-permute-start.5 = (s32[4,2]{1,0:T(4,128)S(1)}, s32[4,2]{1,0:T(4,128)S(1)}, u32[]{:S(2)}, u32[]{:S(2)}) collective-permute-start(s32[4,2]{1,0:T(4,128)S(1)} %get-tuple-element.19.near_ref), channel_id=1, source_target_pairs={{0,4},{1,5},{2,6},{3,7},{4,0},{5,1},{6,2},{7,3},{8,12},{9,13},{10,... | collective-permute-start | bytes 104 | tf_op jit(solution)/shard_map/ppermute | solution.py:240
  32.5 6.0 %collective-permute-start.11 = (f32[2,2,32,128]{3,2,1,0:T(8,128)S(1)}, f32[2,2,32,128]{3,2,1,0:T(8,128)S(1)}, u32[]{:S(2)}, u32[]{:S(2)}) collective-permute-start(f32[2,2,32,128]{3,2,1,0:T(8,128)S(1)} %get-tuple-element.27), channel_id=1, source_target_pairs={{0,3},{1,2},{2,1},{3,0},{4,7},{5,6},{6,5},{7,4},{8,11},{9,10},{10,... | collective-permute-start | bytes 196616 | tf_op jit(solution)/shard_map/ppermute | solution.py:240
  32.5 6.0 %collective-permute-start.12 = (f32[2,2,32,128]{3,2,1,0:T(8,128)S(1)}, f32[2,2,32,128]{3,2,1,0:T(8,128)S(1)}, u32[]{:S(2)}, u32[]{:S(2)}) collective-permute-start(f32[2,2,32,128]{3,2,1,0:T(8,128)S(1)} %get-tuple-element.28), channel_id=1, source_target_pairs={{0,4},{1,5},{2,6},{3,7},{4,0},{5,1},{6,2},{7,3},{8,12},{9,13},{10,... | collective-permute-start | bytes 196616 | tf_op jit(solution)/shard_map/ppermute | solution.py:240
  34.5 4.3 %collective-permute-start.13 = (f32[2,2,32,128]{3,2,1,0:T(8,128)S(1)}, f32[2,2,32,128]{3,2,1,0:T(8,128)S(1)}, u32[]{:S(2)}, u32[]{:S(2)}) collective-permute-start(f32[2,2,32,128]{3,2,1,0:T(8,128)S(1)} %get-tuple-element.29), channel_id=1, source_target_pairs={{0,5},{1,4},{2,7},{3,6},{4,1},{5,0},{6,3},{7,2},{8,13},{9,12},{10,... | collective-permute-start | bytes 196616 | tf_op jit(solution)/shard_map/ppermute | solution.py:240
  34.7 5.5 %collective-permute-start.14 = (f32[2,2,32,128]{3,2,1,0:T(8,128)S(1)}, f32[2,2,32,128]{3,2,1,0:T(8,128)S(1)}, u32[]{:S(2)}, u32[]{:S(2)}) collective-permute-start(f32[2,2,32,128]{3,2,1,0:T(8,128)S(1)} %get-tuple-element.30), channel_id=1, source_target_pairs={{0,6},{1,7},{2,4},{3,5},{4,2},{5,3},{6,0},{7,1},{8,14},{9,15},{10,... | collective-permute-start | bytes 196616 | tf_op jit(solution)/shard_map/ppermute | solution.py:240
  36.1 5.9 %collective-permute-start.15 = (f32[2,2,32,128]{3,2,1,0:T(8,128)S(1)}, f32[2,2,32,128]{3,2,1,0:T(8,128)S(1)}, u32[]{:S(2)}, u32[]{:S(2)}) collective-permute-start(f32[2,2,32,128]{3,2,1,0:T(8,128)S(1)} %get-tuple-element.31), channel_id=1, source_target_pairs={{0,7},{1,6},{2,5},{3,4},{4,3},{5,2},{6,1},{7,0},{8,15},{9,14},{10,... | collective-permute-start | bytes 196616 | tf_op jit(solution)/shard_map/ppermute | solution.py:240
  42.0 9.7 %copy-start.1 = (f32[4,2,32,128]{3,2,1,0:T(8,128)S(1)}, f32[4,2,32,128]{3,2,1,0:T(8,128)}, u32[]{:S(2)}) copy-start(f32[4,2,32,128]{3,2,1,0:T(8,128)} %speed_ref.1) | copy-start | bytes 393220
  42.0 9.7 %copy-start.3 = (f32[4,2,32,128]{3,2,1,0:T(8,128)S(1)}, f32[4,2,32,128]{3,2,1,0:T(8,128)}, u32[]{:S(2)}) copy-start(f32[4,2,32,128]{3,2,1,0:T(8,128)} %density_ref.1) | copy-start | bytes 393220
  42.7 6.5 %collective-permute-start.16 = (f32[2,64,128]{2,1,0:T(8,128)S(1)}, f32[2,64,128]{2,1,0:T(8,128)S(1)}, u32[]{:S(2)}, u32[]{:S(2)}) collective-permute-start(f32[2,64,128]{2,1,0:T(8,128)S(1)} %get-tuple-element.33), channel_id=1, source_target_pairs={{0,8},{8,16},{16,24},{24,0},{1,9},{9,17},{17,25},{25,1},{2,10},{10... | collective-permute-start | bytes 196616 | tf_op jit(solution)/shard_map/ppermute | solution.py:298
  44.3 7.3 %collective-permute-start.17 = (f32[2,64,128]{2,1,0:T(8,128)S(1)}, f32[2,64,128]{2,1,0:T(8,128)S(1)}, u32[]{:S(2)}, u32[]{:S(2)}) collective-permute-start(f32[2,64,128]{2,1,0:T(8,128)S(1)} %get-tuple-element.34), channel_id=1, source_target_pairs={{0,16},{8,24},{16,0},{24,8},{1,17},{9,25},{17,1},{25,9},{2,18},{10... | collective-permute-start | bytes 196616 | tf_op jit(solution)/shard_map/ppermute | solution.py:298
  46.9 4.8 %collective-permute-start.18 = (f32[2,64,128]{2,1,0:T(8,128)S(1)}, f32[2,64,128]{2,1,0:T(8,128)S(1)}, u32[]{:S(2)}, u32[]{:S(2)}) collective-permute-start(f32[2,64,128]{2,1,0:T(8,128)S(1)} %get-tuple-element.35), channel_id=1, source_target_pairs={{0,24},{8,0},{16,8},{24,16},{1,25},{9,1},{17,9},{25,17},{2,26},{10... | collective-permute-start | bytes 196616 | tf_op jit(solution)/shard_map/ppermute | solution.py:298
  51.8 6.3 %collective-permute-start.19 = (f32[2,64,128]{2,1,0:T(8,128)S(1)}, f32[2,64,128]{2,1,0:T(8,128)S(1)}, u32[]{:S(2)}, u32[]{:S(2)}) collective-permute-start(f32[2,64,128]{2,1,0:T(8,128)S(1)} %gradients.1), channel_id=1, source_target_pairs={{0,8},{8,16},{16,24},{24,0},{1,9},{9,17},{17,25},{25,1},{2,10},{10... | collective-permute-start | bytes 196616 | tf_op jit(solution)/shard_map/ppermute | solution.py:298
  53.5 6.7 %collective-permute-start.20 = (f32[2,64,128]{2,1,0:T(8,128)S(1)}, f32[2,64,128]{2,1,0:T(8,128)S(1)}, u32[]{:S(2)}, u32[]{:S(2)}) collective-permute-start(f32[2,64,128]{2,1,0:T(8,128)S(1)} %gradients.1), channel_id=1, source_target_pairs={{0,16},{8,24},{16,0},{24,8},{1,17},{9,25},{17,1},{25,9},{2,18},{10... | collective-permute-start | bytes 196616 | tf_op jit(solution)/shard_map/ppermute | solution.py:298
  55.4 5.0 %collective-permute-start.21 = (f32[2,64,128]{2,1,0:T(8,128)S(1)}, f32[2,64,128]{2,1,0:T(8,128)S(1)}, u32[]{:S(2)}, u32[]{:S(2)}) collective-permute-start(f32[2,64,128]{2,1,0:T(8,128)S(1)} %gradients.1), channel_id=1, source_target_pairs={{0,24},{8,0},{16,8},{24,16},{1,25},{9,1},{17,9},{25,17},{2,26},{10... | collective-permute-start | bytes 196616 | tf_op jit(solution)/shard_map/ppermute | solution.py:298
